TPU v7x, 32 devices: a whole 2x2x4 slice. The times are simulated.
32 devices in a mesh: dp: 4 (over y, core), tile: 8 (over z, x).
Axes of the slice: x: 2, y: 2, z: 4, core: 2. Of those that a mesh axis runs over, the one named last changes fastest.
Arguments:
- inputs: bfloat16 [8, 64, 128, 256], P('dp', None, 'tile'), may hold values from -6 to 6
- cotangent: bfloat16 [8, 64, 128, 256], P('dp', None, 'tile'), may hold values from -6 to 6
- mode_weight: bfloat16 [64, 64, 64, 128], P('tile'), may hold values from -0.5 to 0.5
- local_weight: bfloat16 [64, 64], replicated, may hold values from -0.75 to 0.75
Outputs:
- input_grad: bfloat16 [8, 64, 128, 256], P('dp', None, 'tile')
- mode_grad: float32 [64, 64, 64, 128], P('tile')
- local_grad: float32 [64, 64], replicated
All inputs are finite; a program needn't handle non-finite values.
Results may differ from a plain program's by a relative error of at most 0.015.
Values may be sent and summed in bfloat16 or wider, within the bound.
No kernel may reach another device: no remote copies, remote signals or barrier semaphores. Data moves between devices by JAX's collectives and lax.ppermute only.
A program may use at most 128 MiB of HBM per device.

v0:
```python
import functools
import math

import jax
import jax.numpy as jnp
import numpy as np
from jax import lax
from jax.experimental import pallas as pl
from jax.experimental.pallas import tpu as pltpu
from jax.sharding import PartitionSpec as P

F32 = jnp.float32
BF16 = jnp.bfloat16
LIMIT = 56 * 1024 * 1024
ROWS = 8
PACK = 16
GROUP = 8
SPLIT = 4


def row_tables(height, modes):
    index = np.arange(modes)
    signed = np.where(index < modes // 2, index, index - modes)
    phases = np.mod(np.arange(height)[:, None] * signed[None, :], height)
    angles = phases * (2.0 * math.pi / height)
    return np.cos(angles), np.sin(angles)


def column_tables(width, modes):
    phases = np.mod(np.arange(modes)[:, None] * np.arange(width)[None, :], width)
    angles = phases * (2.0 * math.pi / width)
    return np.stack([np.cos(angles), -np.sin(angles)])


def constant(table):
    return jnp.asarray(np.asarray(table, np.float32)).astype(BF16)


def tables(tiles, owned, th, width, modes):
    cols = column_tables(width, tiles * owned)
    split = cols.reshape(2, tiles, owned, width)
    send_cols = split.transpose(1, 0, 2, 3).reshape(tiles, 2 * owned, width)
    send_cols = np.pad(send_cols, ((0, 0), (0, padded(2 * owned) - 2 * owned), (0, 0))).reshape(-1, width)
    back_cols = split.transpose(2, 1, 0, 3).reshape(-1, width)
    cosine, sine = row_tables(th * tiles, modes)
    real = np.concatenate([cosine, -sine], axis=1)
    imag = np.concatenate([sine, cosine], axis=1)
    pair = np.stack([real, imag]).reshape(2, tiles, th, 2 * modes)
    rows = pair.transpose(2, 1, 0, 3).reshape(-1, 2 * modes)
    back_rows = pair.transpose(1, 0, 2, 3).reshape(-1, 2 * modes)
    return constant(send_cols), constant(rows), constant(back_rows), constant(back_cols)


def padded(rows):
    return -(-rows // PACK) * PACK


def order(outer, inner):
    take = np.arange(outer * inner).reshape(outer, inner).T.reshape(-1)
    return constant(np.eye(outer * inner)[take])


def mode_order(tiles, owned):
    rows = np.arange(tiles * padded(2 * owned)).reshape(tiles, -1)
    take = rows[:, : 2 * owned].reshape(tiles, 2, owned).transpose(2, 0, 1).reshape(-1)
    return constant(np.eye(rows.size)[take])


def dot(left, right, dims):
    return lax.dot_general(left, right, (dims, ((), ())), preferred_element_type=F32)


def low_half(shape, half):
    return lax.broadcasted_iota(jnp.int32, shape, 1) < half


def gelu_slope(values):
    size = jnp.abs(values)
    expo = jnp.exp(-0.5 * values * values)
    t = 1.0 / (1.0 + (0.3275911 / math.sqrt(2.0)) * size)
    poly = 0.5 * 1.061405429
    for factor in (-1.453152027, 1.421413741, -0.284496736, 0.254829592):
        poly = poly * t + 0.5 * factor
    tail = poly * t * expo
    cumulative = jnp.where(values < 0.0, tail, 1.0 - tail)
    return cumulative + values * expo * (1.0 / math.sqrt(2.0 * math.pi))


def shuffle(order_ref, value):
    return dot(order_ref[...], value, ((1,), (0,))).astype(BF16)


def by_rows(order_ref, field_refs, rows_ref):
    heights, lanes, _ = rows_ref.shape
    block = PACK * heights
    quarter = lanes // len(field_refs)
    for first in range(0, lanes, PACK):
        start = first % quarter * heights
        moved = shuffle(order_ref, field_refs[first // quarter][start : start + block, :])
        for h in range(heights):
            rows_ref[h, first : first + PACK, :] = moved[h * PACK : (h + 1) * PACK]


def columns_kernel(order_ref, table_ref, *rest):
    field_refs, (rows_ref, send_ref) = rest[:SPLIT], rest[SPLIT:]
    heights, lanes, _ = rows_ref.shape
    by_rows(order_ref, field_refs, rows_ref)
    for h in range(heights):
        send_ref[:, h * lanes : (h + 1) * lanes] = dot(table_ref[...], rows_ref[h], ((1,), (1,))).astype(BF16)


def relayout_kernel(order_ref, *rest):
    by_rows(order_ref, rest[:SPLIT], rest[SPLIT])


def shuffle_groups(order_ref, recv_ref):
    size = order_ref.shape[0]
    return [shuffle(order_ref, recv_ref[n : n + size, :]) for n in range(0, recv_ref.shape[0], size)]


def stack(groups, index, count, lanes):
    return jnp.concatenate(
        [
            group[index * count : (index + 1) * count, n : n + lanes]
            for n in range(0, groups[0].shape[1], lanes)
            for group in groups
        ],
        axis=0,
    )


def spectra_into(scale, owned, recv_ref, order_ref, rows_ref, spec_ref):
    count = order_ref.shape[0] // owned
    lanes = recv_ref.shape[1] * count // rows_ref.shape[0]
    ordered = [shuffle(order_ref, recv_ref[...])]
    for q in range(owned):
        stacked = stack(ordered, q, count, lanes)
        spec_ref[q * lanes : (q + 1) * lanes, :] = (
            scale * dot(stacked, rows_ref[...], ((0,), (0,)))
        ).astype(BF16)


def grad_spectra_kernel(scale, owned, recv_ref, order_ref, rows_ref, local_ref, spec_ref):
    spectra_into(scale, owned, recv_ref, order_ref, rows_ref, spec_ref)
    value = local_ref[...]
    high = value.astype(BF16)
    low = (value - high.astype(F32)).astype(BF16)
    spec_ref[spec_ref.shape[0] - value.shape[0] :, :] = jnp.concatenate([high, low], axis=1)


def send_inverse(back_ref, mixed, send_ref):
    @pl.when(pl.program_id(0) == pl.num_programs(0) - 1)
    def _():
        owned, lanes, _ = mixed.shape
        for q in range(owned):
            send_ref[:, q * lanes : (q + 1) * lanes] = dot(back_ref[...], mixed[q], ((1,), (1,))).astype(BF16)


def tree(terms):
    while len(terms) > 1:
        terms = [a + b for a, b in zip(terms[0::2], terms[1::2])]
    return terms[0]


def packed_row(store, index):
    row = store[pl.ds(index, 1), :]
    return jnp.broadcast_to(row, (PACK, row.shape[1])).astype(BF16)


def duplicates(spec, half):
    value = spec.astype(F32)
    other = pltpu.roll(value, half, 1)
    low = low_half(value.shape, half)
    return jnp.where(low, value, other), jnp.where(low, other, value)


def forward_kernel(scale, samples, owned, recv_ref, order_ref, rows_ref, back_ref, weight_ref, *rest):
    spec_ref, send_ref, mixed, real, imag, sums = rest
    _, outs, both = sums.shape
    channels = weight_ref.shape[0] // outs
    half = both // 2
    lanes = mixed.shape[1]
    q = pl.program_id(0)

    @pl.when(q == 0)
    def _():
        spectra_into(scale, owned, recv_ref, order_ref, rows_ref, spec_ref)

    spec = spec_ref[pl.ds(pl.multiple_of(q * lanes, lanes), lanes), :]
    real[...], imag[...] = duplicates(spec, half)
    sums[...] = jnp.zeros_like(sums)

    def window(c, o):
        return pl.ds(pl.multiple_of(c * outs + o, PACK), PACK)

    def body(block, carry):
        first = block * GROUP
        rows = [
            [packed_row(store, s * channels + first + step) for step in range(GROUP)]
            for s in range(samples)
            for store in (real, imag)
        ]
        for start in range(0, outs, 2 * PACK):
            totals = []
            for o in (start, start + PACK):
                column = [weight_ref[window(first + step, o), :] for step in range(GROUP)]
                for n, row in enumerate(rows):
                    totals.append((n, o, tree([w * r for w, r in zip(column, row)])))
            updated = [(n, o, sums[n, o : o + PACK, :] + total.astype(F32)) for n, o, total in totals]
            for n, o, total in updated:
                sums[n, o : o + PACK, :] = total
        return carry

    lax.fori_loop(0, channels // GROUP, body, 0)
    low = low_half((outs, both), half)
    result = []
    for s in range(samples):
        crossed = pltpu.roll(sums[2 * s + 1], half, 1)
        result.append(sums[2 * s] + jnp.where(low, -crossed, crossed))
    mixed[q] = jnp.concatenate(result, axis=0).astype(BF16)
    send_inverse(back_ref, mixed, send_ref)


def backward_kernel(samples, spec_ref, back_ref, weight_ref, send_ref, mixed, sums):
    channels, both = sums.shape[1] // ROWS, sums.shape[2]
    outs = weight_ref.shape[0] // channels
    half = both // 2
    lanes = mixed.shape[1]
    q = pl.program_id(0)
    spec = spec_ref[pl.ds(pl.multiple_of(q * lanes, lanes), lanes), :]
    parts = [part.astype(BF16) for part in duplicates(spec, half)]
    grads = [
        [part[s * outs + o : s * outs + o + PACK] for o in range(0, outs, PACK)]
        for s in range(samples)
        for part in parts
    ]

    def window(c, o):
        return pl.ds(pl.multiple_of(c * outs + o, PACK), PACK)

    def body(block, carry):
        totals = []
        for step in range(GROUP // 2):
            c = block * (GROUP // 2) + step
            column = [weight_ref[window(c, o), :] for o in range(0, outs, PACK)]
            for n, grad in enumerate(grads):
                total = tree([w * g for w, g in zip(column, grad)]).astype(F32)
                totals.append((n, c, total[:ROWS] + total[ROWS:]))
        for n, c, total in totals:
            sums[n, pl.ds(pl.multiple_of(c * ROWS, ROWS), ROWS), :] = total
        return carry

    lax.fori_loop(0, channels // (GROUP // 2), body, 0)
    low = low_half((channels, both), half)
    result = []
    for s in range(samples):
        straight, crossed = (
            sum(sums[n, pl.ds(row, channels, stride=ROWS), :] for row in range(ROWS)) for n in (2 * s, 2 * s + 1)
        )
        result.append(jnp.where(low, straight, -straight) + pltpu.roll(crossed, half, 1))
    mixed[q] = jnp.concatenate(result, axis=0).astype(BF16)
    send_inverse(back_ref, mixed, send_ref)


def pixels_kernel(scale, heights, recv_ref, order_ref, back_ref, local_ref, field_ref, cot_ref, table_ref, *rest):
    grad_ref, send_ref, ordered = rest
    steps, lanes, _ = field_ref.shape
    count = order_ref.shape[0] // heights
    size = order_ref.shape[0]
    group = pl.program_id(0)

    @pl.when(group == 0)
    def _():
        for n in range(0, recv_ref.shape[0], size):
            ordered[n : n + size, :] = shuffle(order_ref, recv_ref[n : n + size, :])

    for step in range(steps):
        parts = []
        for n in range(0, recv_ref.shape[0], size):
            first = pl.multiple_of(n + (group * steps + step) * count, count)
            parts.append(ordered[pl.ds(first, count), :])
        inner = stack(parts, 0, count, lanes)
        pre = scale * dot(inner, back_ref[...], ((0,), (0,)))
        pre = pre + dot(local_ref[...], field_ref[step], ((1,), (0,)))
        grad = (cot_ref[step].astype(F32) * gelu_slope(pre)).astype(BF16)
        grad_ref[step] = grad
        send_ref[:, step * lanes : (step + 1) * lanes] = dot(table_ref[...], grad, ((1,), (1,))).astype(BF16)


def local_kernel(samples, field_ref, grad_ref, out_ref):
    heights, lanes, _ = field_ref.shape
    total = jnp.zeros((lanes, lanes), F32)
    for h in range(heights):
        total = total + dot(field_ref[h], grad_ref[h], ((1,), (1,)))
    size = lanes // samples
    out_ref[...] = sum(
        total[s * size : (s + 1) * size, s * size : (s + 1) * size] for s in range(samples)
    )


def final_kernel(scale, recv_ref, order_ref, back_ref, local_ref, grad_ref, restore_ref, out_ref, result):
    heights, lanes, _ = grad_ref.shape
    count = order_ref.shape[0] // heights
    ordered = shuffle_groups(order_ref, recv_ref)
    for h in range(heights):
        inner = stack(ordered, h, count, lanes)
        value = scale * dot(inner, back_ref[...], ((0,), (0,)))
        result[h] = (value + dot(local_ref[...], grad_ref[h], ((1,), (0,)))).astype(BF16)
    block = PACK * heights
    for first in range(0, lanes, PACK):
        part = jnp.concatenate([result[h, first : first + PACK, :] for h in range(heights)], axis=0)
        out_ref[first * heights : first * heights + block, :] = shuffle(restore_ref, part)


def outer_kernel(samples, spec_ref, grad_ref, pair_ref, out_ref, local_ref, real, imag, plain, crossed):
    groups = spec_ref.shape[0]
    total, channels, both = real.shape
    outs = plain.shape[1]
    half = both // 2
    low = low_half((channels, both), half)

    @pl.when(pl.program_id(0) == 0)
    def _():
        pairs = 0.0
        for g in range(groups):
            pair = pair_ref[g].astype(F32)
            pairs = pairs + pair[:, :channels] + pair[:, channels : 2 * channels]
        local_ref[...] = pairs

    for g in range(groups):
        for s in range(samples):
            n = g * samples + s
            spec = spec_ref[g, s * channels : (s + 1) * channels, :].astype(F32)
            other = pltpu.roll(spec, half, 1)
            real[n] = jnp.where(low, spec, other)
            imag[n] = jnp.where(low, other, -spec)
            grad = grad_ref[g, s * outs : (s + 1) * outs, :]
            plain[n] = grad
            crossed[n] = pltpu.roll(grad.astype(F32), half, 1).astype(BF16)

    def body(pair, carry):
        lefts = [
            [packed_row(store.at[n], 2 * pair + c) for n in range(total) for store in (real, imag)] for c in range(2)
        ]
        results = []
        for o in range(0, outs, PACK):
            right = [store[n, o : o + PACK, :] for n in range(total) for store in (plain, crossed)]
            for c, left in enumerate(lefts):
                results.append((c, o, tree([a * b for a, b in zip(left, right)])))
        for c, o, result in results:
            row = pl.multiple_of((2 * pair + c) * outs + o, PACK)
            out_ref[pl.ds(row, PACK), :] = result.astype(F32)
        return carry

    lax.fori_loop(0, channels // 2, body, 0)


def whole(extent):
    return pl.BlockSpec(extent, lambda *_: (0,) * len(extent))


def call(kernel, name, operands, outs, scratch=(), grid=(1,), blocks=None, out_blocks=None):
    blocks, out_blocks = blocks or {}, out_blocks or {}
    in_specs = [blocks.get(n) or whole(operand.shape) for n, operand in enumerate(operands)]
    out_specs = [out_blocks.get(n, whole(out.shape)) for n, out in enumerate(outs)]
    return pl.pallas_call(
        kernel,
        out_shape=tuple(outs),
        grid=grid,
        in_specs=in_specs,
        out_specs=tuple(out_specs),
        scratch_shapes=list(scratch),
        compiler_params=pltpu.CompilerParams(vmem_limit_bytes=LIMIT),
        name=name,
    )(*operands)


def sum_over(values, axis):
    size = lax.axis_size(axis)
    step = 1
    while step < size:
        values = values + lax.ppermute(values, axis, [(i, i ^ step) for i in range(size)])
        step *= 2
    return values


def block_diagonal(matrix, copies):
    zero = jnp.zeros_like(matrix)
    return jnp.concatenate(
        [
            jnp.concatenate([matrix if i == j else zero for j in range(copies)], axis=1)
            for i in range(copies)
        ],
        axis=0,
    )


def shape(extent, kind=BF16):
    return jax.ShapeDtypeStruct(extent, kind)


def local(inputs, cotangent, mode_weight, local_weight):
    tiles = lax.axis_size("tile")
    samples, channels, th, width = inputs.shape
    owned, _, _, both = mode_weight.shape
    modes = both // 2
    lanes = samples * channels
    parts = width // 128
    spec_scale = 1.0 / math.sqrt(tiles * th * width)
    mode_scale = 1.0 / math.sqrt(modes * tiles * owned)
    send_cols, rows, back_rows, back_cols = tables(tiles, owned, th, width, modes)
    pixel_rows = samples * channels * th
    halves = tiles * padded(2 * owned)
    inverse = 2 * tiles * th

    def exchange(values):
        split = values.reshape(tiles, values.shape[0] // tiles, values.shape[1])
        moved = lax.all_to_all(split, "tile", split_axis=0, concat_axis=0, tiled=False)
        return moved.reshape(values.shape)

    forward_mix = block_diagonal(local_weight.T, samples)
    backward_mix = block_diagonal(local_weight, samples)
    by_row = order(PACK, th)
    by_channel = order(th, PACK)
    by_mode = mode_order(tiles, owned)
    by_height = order(2 * min(tiles, 8), th)
    mixed = pltpu.VMEM((owned, lanes, both), BF16)
    flat_weight = mode_weight.reshape(-1, both)
    weight_block = pl.BlockSpec((flat_weight.shape[0] // owned, both), lambda q: (q, 0))
    to_modes = shape((halves, th * lanes))
    to_pixels = shape((inverse, owned * lanes))
    field_shape = shape((th, lanes, width))

    def field_blocks(first):
        return {first + n: pl.BlockSpec((pixel_rows // SPLIT, width), lambda _, n=n: (n, 0)) for n in range(SPLIT)}

    field_rows, send = call(
        columns_kernel,
        "columns",
        (by_row, send_cols, *[inputs.reshape(pixel_rows, width)] * SPLIT),
        (field_shape, to_modes),
        blocks=field_blocks(2),
    )
    arrived = exchange(send)
    (cot_rows,) = call(
        relayout_kernel,
        "relayout",
        (by_row, *[cotangent.reshape(pixel_rows, width)] * SPLIT),
        (field_shape,),
        blocks=field_blocks(1),
    )
    spectra, send = call(
        functools.partial(forward_kernel, spec_scale, samples, owned),
        "mix_forward",
        (arrived, by_mode, rows, back_rows, flat_weight),
        (shape((owned * lanes, both)), to_pixels),
        [
            mixed,
            pltpu.VMEM((lanes, both), F32),
            pltpu.VMEM((lanes, both), F32),
            pltpu.VMEM((2 * samples, channels, both), F32),
        ],
        grid=(owned,),
        blocks={4: weight_block},
    )
    all_spectra = lax.all_gather(spectra, "dp")
    arrived = exchange(send)
    steps = 4
    row_block = pl.BlockSpec((steps, lanes, width), lambda n: (n, 0, 0))
    gate_rows, send = call(
        functools.partial(pixels_kernel, mode_scale, th),
        "pixels",
        (arrived, by_height, back_cols, forward_mix, field_rows, cot_rows, send_cols),
        (field_shape, to_modes),
        [pltpu.VMEM((inverse, owned * lanes), BF16)],
        grid=(th // steps,),
        blocks={4: row_block, 5: row_block},
        out_blocks={0: row_block, 1: pl.BlockSpec((halves, steps * lanes), lambda n: (0, n))},
    )
    arrived = exchange(send)
    (local_sum,) = call(
        functools.partial(local_kernel, samples),
        "local_grad",
        (field_rows, gate_rows),
        (shape((channels, channels), F32),),
    )
    local_sum = sum_over(local_sum, "tile")
    (grad_spectra,) = call(
        functools.partial(grad_spectra_kernel, mode_scale, owned),
        "grad_spectra",
        (arrived, by_mode, rows, local_sum),
        (shape((owned * lanes + channels, both)),),
    )
    all_grads = lax.all_gather(grad_spectra, "dp")
    (send,) = call(
        functools.partial(backward_kernel, samples),
        "mix_backward",
        (grad_spectra, back_rows, flat_weight),
        (to_pixels,),
        [mixed, pltpu.VMEM((2 * samples, channels * ROWS, both), F32)],
        grid=(owned,),
        blocks={2: weight_block},
    )
    arrived = exchange(send)

    groups = lax.axis_size("dp")
    total = groups * samples
    per_mode = pl.BlockSpec((groups, lanes, both), lambda q: (0, q, 0))
    below = owned * lanes // channels
    mode_grad, local_grad = call(
        functools.partial(outer_kernel, samples),
        "mode_grad",
        (all_spectra, all_grads, all_grads),
        (shape(flat_weight.shape, F32), shape((channels, channels), F32)),
        [pltpu.VMEM((total, channels, both), F32)] * 2 + [pltpu.VMEM((total, channels, both), BF16)] * 2,
        grid=(owned,),
        blocks={
            0: per_mode,
            1: per_mode,
            2: pl.BlockSpec((groups, channels, both), lambda q: (0, below, 0)),
        },
        out_blocks={0: weight_block},
    )
    arrived, mode_grad = lax.optimization_barrier((arrived, mode_grad))

    (input_grad,) = call(
        functools.partial(final_kernel, spec_scale),
        "final",
        (arrived, by_height, back_cols, backward_mix, gate_rows, by_channel),
        (shape((pixel_rows, width)),),
        [pltpu.VMEM((th, lanes, width), BF16)],
    )
    return (input_grad.reshape(inputs.shape), mode_grad.reshape(mode_weight.shape), local_grad)


def solution(mesh):
    return jax.shard_map(
        local,
        mesh=mesh,
        in_specs=(
            P("dp", None, "tile", None),
            P("dp", None, "tile", None),
            P("tile", None, None, None),
            P(),
        ),
        out_specs=(P("dp", None, "tile", None), P("tile", None, None, None), P()),
        check_vma=False,
    )
```

profile of v0, /device:TPU:0, one launch (start us, length us, event | category | flops | bytes accessed | tf_op | source)
XLA Modules:
  0.0 143.4 jit_solution(10351985879281231487)
XLA Ops:
  7.2 2.9 %columns.1 = (bf16[16,128,256]{2,1,0:T(8,128)(2,1)}, bf16[128,2048]{1,0:T(8,128)(2,1)}) custom-call(bf16[256,256]{1,0:T(8,128)(2,1)} %constant.30.order_ref.restore_ref, bf16[128,256]{1,0:T(8,128)(2,1)} %constant.31.table_ref, bf16[2048,256]{1,0:T(8,128)(2,1)} %bitcast.18, bf16[2048,256]{1,0:T(8,128)(2,1)} %bitcast.19, bf16[2048,256]{1,0:T(8,128)(2,1)} %bitcast.20, ...), custom_call_target="tpu_custom_call" | custom-call | tf_op jit(solution)/shard_map/columns/pallas_call | solution.py:366
  10.1 0.0 copy-start.3
  10.1 22.0 %all_to_all.20 = bf16[8,16,2048]{2,1,0:T(8,128)(2,1)} all-to-all(bf16[8,16,2048]{2,1,0:T(8,128)(2,1)} %bitcast.37), channel_id=1, replica_groups=mesh['dp'=4,'tile'=8] {'tile'}, dimensions={0} | all-to-all | bytes 1048576 | tf_op jit(solution)/shard_map/all_to_all | solution.py:418
  32.1 11.4 %mix_forward.1 = (bf16[1024,128]{1,0:T(8,128)(2,1)}, bf16[256,1024]{1,0:T(8,128)(2,1)}) custom-call(bf16[128,2048]{1,0:T(8,128)(2,1)} %bitcast.29, bf16[128,128]{1,0:T(8,128)(2,1)} %constant.32.order_ref, bf16[256,128]{1,0:T(8,128)(2,1)} %constant.33.rows_ref, bf16[256,128]{1,0:T(8,128)(2,1)} %constant.34.back_ref, bf16[32768,128]{1,0:T(8,128)(2,1)} %bitcast.16), custom_call_target="tpu_custom_call" | custom-call | tf_op jit(solution)/shard_map/mix_forward/pallas_call | solution.py:366
  43.5 3.6 %all-to-all-start.1 = ((bf16[8,32,1024]{2,1,0:T(8,128)(2,1)}), bf16[8,32,1024]{2,1,0:T(8,128)(2,1)S(1)}, u32[]{:S(2)}, u32[]{:S(2)}) async-start(bf16[8,32,1024]{2,1,0:T(8,128)(2,1)} %bitcast.36), calls=%async_computation.1 | async-start | bytes 1048576 | tf_op jit(solution)/shard_map/all_to_all | solution.py:418
  47.1 0.0 all-gather.5.cloned.1.call-start
  47.1 0.7 all-gather.5.cloned.1.call-update
  47.8 2.6 %relayout.1.cot_ref = bf16[16,128,256]{2,1,0:T(8,128)(2,1)} custom-call(bf16[256,256]{1,0:T(8,128)(2,1)} %constant.30.order_ref.restore_ref, bf16[2048,256]{1,0:T(8,128)(2,1)} %bitcast.22, bf16[2048,256]{1,0:T(8,128)(2,1)} %bitcast.23, bf16[2048,256]{1,0:T(8,128)(2,1)} %bitcast.24, bf16[2048,256]{1,0:T(8,128)(2,1)} %bitcast.25), custom_call_target="tpu_custom_call" | custom-call | tf_op jit(solution)/shard_map/relayout/pallas_call | solution.py:366
  50.4 0.0 copy-done.3
  50.4 0.1 copy.15
  50.5 0.7 fusion.4.local_ref
  51.2 10.0 %all-to-all-done.1 = bf16[8,32,1024]{2,1,0:T(8,128)(2,1)S(1)} async-done(((bf16[8,32,1024]{2,1,0:T(8,128)(2,1)}), bf16[8,32,1024]{2,1,0:T(8,128)(2,1)S(1)}, u32[]{:S(2)}, u32[]{:S(2)}) %all-to-all-start.1) | async-done | bytes 524320 | tf_op jit(solution)/shard_map/all_to_all | solution.py:418
  61.2 0.0 copy-start.1
  61.3 0.8 copy-done.1
  62.1 7.7 %pixels.1 = (bf16[16,128,256]{2,1,0:T(8,128)(2,1)}, bf16[128,2048]{1,0:T(8,128)(2,1)}) custom-call(bf16[256,1024]{1,0:T(8,128)(2,1)} %bitcast.31, bf16[256,256]{1,0:T(8,128)(2,1)} %constant.30.order_ref.restore_ref, bf16[128,256]{1,0:T(8,128)(2,1)} %constant.35.back_ref, bf16[128,128]{1,0:T(8,128)(2,1)} %fusion.4.local_ref, ...), custom_call_target="tpu_custom_call" | custom-call | tf_op jit(solution)/shard_map/pixels/pallas_call | solution.py:366
  69.7 3.6 %all-to-all-start.2 = ((bf16[8,16,2048]{2,1,0:T(8,128)(2,1)}), bf16[8,16,2048]{2,1,0:T(8,128)(2,1)S(1)}, u32[]{:S(2)}, u32[]{:S(2)}) async-start(bf16[8,16,2048]{2,1,0:T(8,128)(2,1)} %bitcast.35), calls=%async_computation.2 | async-start | bytes 1048576 | tf_op jit(solution)/shard_map/all_to_all | solution.py:418
  73.4 0.0 all-gather.7.cloned.1.call-start
  73.4 2.7 %local_grad.1 = f32[64,64]{1,0:T(8,128)} custom-call(bf16[16,128,256]{2,1,0:T(8,128)(2,1)} %get-tuple-element.15.field_ref, bf16[16,128,256]{2,1,0:T(8,128)(2,1)} %get-tuple-element.17.grad_ref), custom_call_target="tpu_custom_call" | custom-call | tf_op jit(solution)/shard_map/local_grad/pallas_call | solution.py:366
  76.1 2.0 %collective-permute-start = (f32[64,64]{1,0:T(8,128)}, f32[64,64]{1,0:T(8,128)S(1)}, u32[]{:S(2)}, u32[]{:S(2)}) collective-permute-start(f32[64,64]{1,0:T(8,128)} %local_grad.1), channel_id=1, source_target_pairs={{0,1},{1,0},{2,3},{3,2},{4,5},{5,4},{6,7},{7,6},{8,9},{9,8},{10,11... | collective-permute-start | bytes 49160 | tf_op jit(solution)/shard_map/ppermute | solution.py:382
  78.0 2.7 %collective-permute-done = f32[64,64]{1,0:T(8,128)S(1)} collective-permute-done((f32[64,64]{1,0:T(8,128)}, f32[64,64]{1,0:T(8,128)S(1)}, u32[]{:S(2)}, u32[]{:S(2)}) %collective-permute-start) | collective-permute-done | bytes 16416 | tf_op jit(solution)/shard_map/ppermute | solution.py:382
  80.8 0.8 add.17
  81.5 2.5 %collective-permute-start.1 = (f32[64,64]{1,0:T(8,128)S(1)}, f32[64,64]{1,0:T(8,128)S(1)}, u32[]{:S(2)}, u32[]{:S(2)}) collective-permute-start(f32[64,64]{1,0:T(8,128)S(1)} %add.17), channel_id=1, source_target_pairs={{0,2},{1,3},{2,0},{3,1},{4,6},{5,7},{6,4},{7,5},{8,10},{9,11},{10,... | collective-permute-start | bytes 49160 | tf_op jit(solution)/shard_map/ppermute | solution.py:382
  84.1 1.9 %collective-permute-done.1 = f32[64,64]{1,0:T(8,128)S(1)} collective-permute-done((f32[64,64]{1,0:T(8,128)S(1)}, f32[64,64]{1,0:T(8,128)S(1)}, u32[]{:S(2)}, u32[]{:S(2)}) %collective-permute-start.1) | collective-permute-done | bytes 16416 | tf_op jit(solution)/shard_map/ppermute | solution.py:382
  86.0 2.0 %collective-permute-start.2 = (f32[64,64]{1,0:T(8,128)S(1)}, f32[64,64]{1,0:T(8,128)S(1)}, u32[]{:S(2)}, u32[]{:S(2)}) collective-permute-start(f32[64,64]{1,0:T(8,128)S(1)} %add.18), channel_id=1, source_target_pairs={{0,4},{1,5},{2,6},{3,7},{4,0},{5,1},{6,2},{7,3},{8,12},{9,13},{10,... | collective-permute-start | bytes 49160 | tf_op jit(solution)/shard_map/ppermute | solution.py:382
  87.9 2.9 %collective-permute-done.2 = f32[64,64]{1,0:T(8,128)S(1)} collective-permute-done((f32[64,64]{1,0:T(8,128)S(1)}, f32[64,64]{1,0:T(8,128)S(1)}, u32[]{:S(2)}, u32[]{:S(2)}) %collective-permute-start.2) | collective-permute-done | bytes 16416 | tf_op jit(solution)/shard_map/ppermute | solution.py:382
  90.9 0.6 add.19.local_ref
  91.5 0.0 all-to-all-done.2
  91.5 0.0 copy-start
  91.5 0.8 copy-done
  92.3 2.4 %grad_spectra.1.spec_ref = bf16[1088,128]{1,0:T(8,128)(2,1)} custom-call(bf16[128,2048]{1,0:T(8,128)(2,1)} %bitcast.30, bf16[128,128]{1,0:T(8,128)(2,1)} %constant.32.order_ref, bf16[256,128]{1,0:T(8,128)(2,1)} %constant.33.rows_ref, f32[64,64]{1,0:T(8,128)} %add.19.local_ref), custom_call_target="tpu_custom_call" | custom-call | tf_op jit(solution)/shard_map/grad_spectra/pallas_call | solution.py:366
  94.7 0.0 all-gather.7.cloned.1.call-update
  94.7 11.2 %mix_backward.1 = bf16[256,1024]{1,0:T(8,128)(2,1)} custom-call(bf16[1088,128]{1,0:T(8,128)(2,1)} %grad_spectra.1.spec_ref, bf16[256,128]{1,0:T(8,128)(2,1)} %constant.34.back_ref, bf16[32768,128]{1,0:T(8,128)(2,1)} %bitcast.17), custom_call_target="tpu_custom_call" | custom-call | tf_op jit(solution)/shard_map/mix_backward/pallas_call | solution.py:366
  105.9 5.8 %all-to-all-start.3 = ((bf16[8,32,1024]{2,1,0:T(8,128)(2,1)}), bf16[8,32,1024]{2,1,0:T(8,128)(2,1)S(1)}, u32[]{:S(2)}, u32[]{:S(2)}) async-start(bf16[8,32,1024]{2,1,0:T(8,128)(2,1)} %bitcast.28), calls=%async_computation.3 | async-start | bytes 1048576 | tf_op jit(solution)/shard_map/all_to_all | solution.py:418
  111.6 0.7 fusion.5.local_ref
  112.3 0.0 all-gather.5.cloned.1.call-done
  112.3 0.8 all-gather.7.cloned.1.call-done
  113.1 18.8 %mode_grad.1 = (f32[32768,128]{1,0:T(8,128)}, f32[64,64]{1,0:T(8,128)}) custom-call(bf16[4,1024,128]{2,1,0:T(8,128)(2,1)} %bitcast.33, bf16[4,1088,128]{2,1,0:T(8,128)(2,1)} %bitcast.26, bf16[4,1088,128]{2,1,0:T(8,128)(2,1)} %bitcast.27), custom_call_target="tpu_custom_call" | custom-call | tf_op jit(solution)/shard_map/mode_grad/pallas_call | solution.py:366
  131.9 0.0 all-to-all-done.3
  132.0 0.0 copy-start.2
  132.0 0.8 copy-done.2
  132.8 3.8 %final.1 = bf16[2048,256]{1,0:T(8,128)(2,1)} custom-call(bf16[256,1024]{1,0:T(8,128)(2,1)} %bitcast.32, bf16[256,256]{1,0:T(8,128)(2,1)} %constant.30.order_ref.restore_ref, bf16[128,256]{1,0:T(8,128)(2,1)} %constant.35.back_ref, bf16[128,128]{1,0:T(8,128)(2,1)} %fusion.5.local_ref, bf16[16,128,256]{2,1,0:T(8,128)(2,1)} %get-tuple-element.17.grad_ref, ...), custom_call_target="tpu_custom_call" | custom-call | tf_op jit(solution)/shard_map/final/pallas_call | solution.py:366
  (1 shorter events, 0.0 us)
Async XLA Ops:
  10.1 40.4 %copy-start.3 = (bf16[64,64]{1,0:T(8,128)(2,1)S(1)}, bf16[64,64]{1,0:T(8,128)(2,1)}, u32[]{:S(2)}) copy-start(bf16[64,64]{1,0:T(8,128)(2,1)} %param.15) | copy-start | bytes 24580
  43.5 17.8 %all-to-all-start.1 = ((bf16[8,32,1024]{2,1,0:T(8,128)(2,1)}), bf16[8,32,1024]{2,1,0:T(8,128)(2,1)S(1)}, u32[]{:S(2)}, u32[]{:S(2)}) async-start(bf16[8,32,1024]{2,1,0:T(8,128)(2,1)} %bitcast.36), calls=%async_computation.1 | async-start | bytes 1048576 | tf_op jit(solution)/shard_map/all_to_all | solution.py:418
  47.1 65.2 %all-gather.5.cloned.1.call-start = ((), (), s32[]{:S(2)}) async-start(), calls=%async_computation.4 | async-start | bytes 1310720 | tf_op jit(solution)/shard_map/all_gather | solution.py:466
  61.2 0.8 copy-start.1
  69.7 21.8 %all-to-all-start.2 = ((bf16[8,16,2048]{2,1,0:T(8,128)(2,1)}), bf16[8,16,2048]{2,1,0:T(8,128)(2,1)S(1)}, u32[]{:S(2)}, u32[]{:S(2)}) async-start(bf16[8,16,2048]{2,1,0:T(8,128)(2,1)} %bitcast.35), calls=%async_computation.2 | async-start | bytes 1048576 | tf_op jit(solution)/shard_map/all_to_all | solution.py:418
  73.4 39.8 %all-gather.7.cloned.1.call-start = ((), (), s32[]{:S(2)}) async-start(), calls=%async_computation.5 | async-start | bytes 1392640 | tf_op jit(solution)/shard_map/all_gather | solution.py:494
  76.1 4.7 %collective-permute-start = (f32[64,64]{1,0:T(8,128)}, f32[64,64]{1,0:T(8,128)S(1)}, u32[]{:S(2)}, u32[]{:S(2)}) collective-permute-start(f32[64,64]{1,0:T(8,128)} %local_grad.1), channel_id=1, source_target_pairs={{0,1},{1,0},{2,3},{3,2},{4,5},{5,4},{6,7},{7,6},{8,9},{9,8},{10,11... | collective-permute-start | bytes 49160 | tf_op jit(solution)/shard_map/ppermute | solution.py:382
  81.5 4.4 %collective-permute-start.1 = (f32[64,64]{1,0:T(8,128)S(1)}, f32[64,64]{1,0:T(8,128)S(1)}, u32[]{:S(2)}, u32[]{:S(2)}) collective-permute-start(f32[64,64]{1,0:T(8,128)S(1)} %add.17), channel_id=1, source_target_pairs={{0,2},{1,3},{2,0},{3,1},{4,6},{5,7},{6,4},{7,5},{8,10},{9,11},{10,... | collective-permute-start | bytes 49160 | tf_op jit(solution)/shard_map/ppermute | solution.py:382
  86.0 4.9 %collective-permute-start.2 = (f32[64,64]{1,0:T(8,128)S(1)}, f32[64,64]{1,0:T(8,128)S(1)}, u32[]{:S(2)}, u32[]{:S(2)}) collective-permute-start(f32[64,64]{1,0:T(8,128)S(1)} %add.18), channel_id=1, source_target_pairs={{0,4},{1,5},{2,6},{3,7},{4,0},{5,1},{6,2},{7,3},{8,12},{9,13},{10,... | collective-permute-start | bytes 49160 | tf_op jit(solution)/shard_map/ppermute | solution.py:382
  91.5 0.8 copy-start
  105.9 26.1 %all-to-all-start.3 = ((bf16[8,32,1024]{2,1,0:T(8,128)(2,1)}), bf16[8,32,1024]{2,1,0:T(8,128)(2,1)S(1)}, u32[]{:S(2)}, u32[]{:S(2)}) async-start(bf16[8,32,1024]{2,1,0:T(8,128)(2,1)} %bitcast.28), calls=%async_computation.3 | async-start | bytes 1048576 | tf_op jit(solution)/shard_map/all_to_all | solution.py:418
  132.0 0.8 copy-start.2
Sparse Core Ops, SparseCore 0:
  49.5 18.1 all-gather.4
  94.8 18.2 all-gather.6
where the time goes:
time: 144 us; the launch traced here: 143 us
  Pallas kernels  63.4 us (44%)
  blocking collectives  22 us (15%)
  starting transfers between devices  19.5 us (14%)
  waiting for transfers between devices  19.1 us (13%)
  between operations  14.1 us (10%)
  other arithmetic  2.77 us (2%)
  local copies, waits for them, and re-layouts  2.51 us (2%)
    pallas_call x9, Pallas kernels, call(): pl.pallas_call(kernel, out_shape=tuple(outs), grid=grid, in_specs=in_spec...  63.4 us
    all_to_all x1, blocking collectives, exchange(): lax.all_to_all(split, 'tile', split_axis=0, concat_axis=0, tiled=False)  22 us
    all_to_all x3, starting transfers between devices, exchange(): lax.all_to_all(split, 'tile', split_axis=0, concat_axis=0, tiled=False)  13 us
    all_to_all x3, waiting for transfers between devices, exchange(): lax.all_to_all(split, 'tile', split_axis=0, concat_axis=0, tiled=False)  10 us
    ppermute x3, waiting for transfers between devices, sum_over(): lax.ppermute(values, axis, [(i, i ^ step) for i in range(size)])  7.56 us
    ppermute x3, starting transfers between devices, sum_over(): lax.ppermute(values, axis, [(i, i ^ step) for i in range(size)])  6.46 us
  transfers between devices with their start and end apart: 8, of which 5 were waited for; matrix products, arithmetic and copies ran while one was open for 2% of the time, Pallas kernels for 32%

commit v1 on v0

--- a/solution.py
+++ b/solution.py
@@ -12,6 +12,7 @@
 F32 = jnp.float32
 BF16 = jnp.bfloat16
 LIMIT = 56 * 1024 * 1024
+SMALL = 24 * 1024 * 1024
 ROWS = 8
 PACK = 16
 GROUP = 8
@@ -148,14 +149,6 @@
     spec_ref[spec_ref.shape[0] - value.shape[0] :, :] = jnp.concatenate([high, low], axis=1)
 
 
-def send_inverse(back_ref, mixed, send_ref):
-    @pl.when(pl.program_id(0) == pl.num_programs(0) - 1)
-    def _():
-        owned, lanes, _ = mixed.shape
-        for q in range(owned):
-            send_ref[:, q * lanes : (q + 1) * lanes] = dot(back_ref[...], mixed[q], ((1,), (1,))).astype(BF16)
-
-
 def tree(terms):
     while len(terms) > 1:
         terms = [a + b for a, b in zip(terms[0::2], terms[1::2])]
@@ -174,21 +167,29 @@
     return jnp.where(low, value, other), jnp.where(low, other, value)
 
 
+def finish(back_ref, sums, send_ref, mix):
+    @pl.when(pl.program_id(0) == pl.num_programs(0) - 1)
+    def _():
+        owned = sums.shape[0]
+        lanes = send_ref.shape[1] // owned
+        for q in range(owned):
+            mixed = mix(sums.at[q]).astype(BF16)
+            send_ref[:, q * lanes : (q + 1) * lanes] = dot(back_ref[...], mixed, ((1,), (1,))).astype(BF16)
+
+
 def forward_kernel(scale, samples, owned, recv_ref, order_ref, rows_ref, back_ref, weight_ref, *rest):
-    spec_ref, send_ref, mixed, real, imag, sums = rest
-    _, outs, both = sums.shape
+    spec_ref, send_ref, real, imag, sums = rest
+    _, _, outs, both = sums.shape
     channels = weight_ref.shape[0] // outs
     half = both // 2
-    lanes = mixed.shape[1]
+    lanes = samples * channels
     q = pl.program_id(0)
 
     @pl.when(q == 0)
     def _():
         spectra_into(scale, owned, recv_ref, order_ref, rows_ref, spec_ref)
-
-    spec = spec_ref[pl.ds(pl.multiple_of(q * lanes, lanes), lanes), :]
-    real[...], imag[...] = duplicates(spec, half)
-    sums[...] = jnp.zeros_like(sums)
+        real[...], imag[...] = duplicates(spec_ref[...], half)
+        sums[...] = jnp.zeros_like(sums)
 
     def window(c, o):
         return pl.ds(pl.multiple_of(c * outs + o, PACK), PACK)
@@ -196,7 +197,7 @@
     def body(block, carry):
         first = block * GROUP
         rows = [
-            [packed_row(store, s * channels + first + step) for step in range(GROUP)]
+            [packed_row(store, q * lanes + s * channels + first + step) for step in range(GROUP)]
             for s in range(samples)
             for store in (real, imag)
         ]
@@ -206,33 +207,40 @@
                 column = [weight_ref[window(first + step, o), :] for step in range(GROUP)]
                 for n, row in enumerate(rows):
                     totals.append((n, o, tree([w * r for w, r in zip(column, row)])))
-            updated = [(n, o, sums[n, o : o + PACK, :] + total.astype(F32)) for n, o, total in totals]
+            updated = [(n, o, sums[q, n, o : o + PACK, :] + total.astype(F32)) for n, o, total in totals]
             for n, o, total in updated:
-                sums[n, o : o + PACK, :] = total
+                sums[q, n, o : o + PACK, :] = total
         return carry
 
     lax.fori_loop(0, channels // GROUP, body, 0)
-    low = low_half((outs, both), half)
-    result = []
-    for s in range(samples):
-        crossed = pltpu.roll(sums[2 * s + 1], half, 1)
-        result.append(sums[2 * s] + jnp.where(low, -crossed, crossed))
-    mixed[q] = jnp.concatenate(result, axis=0).astype(BF16)
-    send_inverse(back_ref, mixed, send_ref)
-
-
-def backward_kernel(samples, spec_ref, back_ref, weight_ref, send_ref, mixed, sums):
-    channels, both = sums.shape[1] // ROWS, sums.shape[2]
+
+    def mix(parts):
+        low = low_half((outs, both), half)
+        result = []
+        for s in range(samples):
+            crossed = pltpu.roll(parts[2 * s + 1], half, 1)
+            result.append(parts[2 * s] + jnp.where(low, -crossed, crossed))
+        return jnp.concatenate(result, axis=0)
+
+    finish(back_ref, sums, send_ref, mix)
+
+
+def backward_kernel(samples, spec_ref, back_ref, weight_ref, send_ref, real, imag, sums):
+    channels, both = sums.shape[2] // ROWS, sums.shape[3]
     outs = weight_ref.shape[0] // channels
     half = both // 2
-    lanes = mixed.shape[1]
+    lanes = samples * outs
     q = pl.program_id(0)
-    spec = spec_ref[pl.ds(pl.multiple_of(q * lanes, lanes), lanes), :]
-    parts = [part.astype(BF16) for part in duplicates(spec, half)]
+
+    @pl.when(q == 0)
+    def _():
+        first, second = duplicates(spec_ref[: real.shape[0], :], half)
+        real[...], imag[...] = first.astype(BF16), second.astype(BF16)
+
     grads = [
-        [part[s * outs + o : s * outs + o + PACK] for o in range(0, outs, PACK)]
+        [store[pl.ds(pl.multiple_of(q * lanes + s * outs + o, PACK), PACK), :] for o in range(0, outs, PACK)]
         for s in range(samples)
-        for part in parts
+        for store in (real, imag)
     ]
 
     def window(c, o):
@@ -240,30 +248,33 @@
 
     def body(block, carry):
         totals = []
-        for step in range(GROUP // 2):
-            c = block * (GROUP // 2) + step
+        for step in range(GROUP):
+            c = block * GROUP + step
             column = [weight_ref[window(c, o), :] for o in range(0, outs, PACK)]
             for n, grad in enumerate(grads):
                 total = tree([w * g for w, g in zip(column, grad)]).astype(F32)
                 totals.append((n, c, total[:ROWS] + total[ROWS:]))
         for n, c, total in totals:
-            sums[n, pl.ds(pl.multiple_of(c * ROWS, ROWS), ROWS), :] = total
+            sums[q, n, pl.ds(pl.multiple_of(c * ROWS, ROWS), ROWS), :] = total
         return carry
 
-    lax.fori_loop(0, channels // (GROUP // 2), body, 0)
-    low = low_half((channels, both), half)
-    result = []
-    for s in range(samples):
-        straight, crossed = (
-            sum(sums[n, pl.ds(row, channels, stride=ROWS), :] for row in range(ROWS)) for n in (2 * s, 2 * s + 1)
-        )
-        result.append(jnp.where(low, straight, -straight) + pltpu.roll(crossed, half, 1))
-    mixed[q] = jnp.concatenate(result, axis=0).astype(BF16)
-    send_inverse(back_ref, mixed, send_ref)
+    lax.fori_loop(0, channels // GROUP, body, 0)
+
+    def mix(parts):
+        low = low_half((channels, both), half)
+        result = []
+        for s in range(samples):
+            straight, crossed = (
+                sum(parts[n, pl.ds(row, channels, stride=ROWS), :] for row in range(ROWS)) for n in (2 * s, 2 * s + 1)
+            )
+            result.append(jnp.where(low, straight, -straight) + pltpu.roll(crossed, half, 1))
+        return jnp.concatenate(result, axis=0)
+
+    finish(back_ref, sums, send_ref, mix)
 
 
 def pixels_kernel(scale, heights, recv_ref, order_ref, back_ref, local_ref, field_ref, cot_ref, table_ref, *rest):
-    grad_ref, send_ref, ordered = rest
+    grad_ref, send_ref, sum_ref, ordered, total = rest
     steps, lanes, _ = field_ref.shape
     count = order_ref.shape[0] // heights
     size = order_ref.shape[0]
@@ -273,7 +284,9 @@
     def _():
         for n in range(0, recv_ref.shape[0], size):
             ordered[n : n + size, :] = shuffle(order_ref, recv_ref[n : n + size, :])
-
+        total[...] = jnp.zeros_like(total)
+
+    local = jnp.zeros(total.shape, F32)
     for step in range(steps):
         parts = []
         for n in range(0, recv_ref.shape[0], size):
@@ -285,17 +298,13 @@
         grad = (cot_ref[step].astype(F32) * gelu_slope(pre)).astype(BF16)
         grad_ref[step] = grad
         send_ref[:, step * lanes : (step + 1) * lanes] = dot(table_ref[...], grad, ((1,), (1,))).astype(BF16)
-
-
-def local_kernel(samples, field_ref, grad_ref, out_ref):
-    heights, lanes, _ = field_ref.shape
-    total = jnp.zeros((lanes, lanes), F32)
-    for h in range(heights):
-        total = total + dot(field_ref[h], grad_ref[h], ((1,), (1,)))
-    size = lanes // samples
-    out_ref[...] = sum(
-        total[s * size : (s + 1) * size, s * size : (s + 1) * size] for s in range(samples)
-    )
+        local = local + dot(field_ref[step], grad, ((1,), (1,)))
+    total[...] += local
+
+    @pl.when(group == pl.num_programs(0) - 1)
+    def _():
+        extent = sum_ref.shape[0]
+        sum_ref[...] = sum(total[n : n + extent, n : n + extent] for n in range(0, lanes, extent))
 
 
 def final_kernel(scale, recv_ref, order_ref, back_ref, local_ref, grad_ref, restore_ref, out_ref, result):
@@ -359,7 +368,7 @@
     return pl.BlockSpec(extent, lambda *_: (0,) * len(extent))
 
 
-def call(kernel, name, operands, outs, scratch=(), grid=(1,), blocks=None, out_blocks=None):
+def call(kernel, name, operands, outs, scratch=(), grid=(1,), blocks=None, out_blocks=None, limit=LIMIT):
     blocks, out_blocks = blocks or {}, out_blocks or {}
     in_specs = [blocks.get(n) or whole(operand.shape) for n, operand in enumerate(operands)]
     out_specs = [out_blocks.get(n, whole(out.shape)) for n, out in enumerate(outs)]
@@ -370,7 +379,7 @@
         in_specs=in_specs,
         out_specs=tuple(out_specs),
         scratch_shapes=list(scratch),
-        compiler_params=pltpu.CompilerParams(vmem_limit_bytes=LIMIT),
+        compiler_params=pltpu.CompilerParams(vmem_limit_bytes=limit),
         name=name,
     )(*operands)
 
@@ -424,7 +433,6 @@
     by_channel = order(th, PACK)
     by_mode = mode_order(tiles, owned)
     by_height = order(2 * min(tiles, 8), th)
-    mixed = pltpu.VMEM((owned, lanes, both), BF16)
     flat_weight = mode_weight.reshape(-1, both)
     weight_block = pl.BlockSpec((flat_weight.shape[0] // owned, both), lambda q: (q, 0))
     to_modes = shape((halves, th * lanes))
@@ -455,10 +463,9 @@
         (arrived, by_mode, rows, back_rows, flat_weight),
         (shape((owned * lanes, both)), to_pixels),
         [
-            mixed,
-            pltpu.VMEM((lanes, both), F32),
-            pltpu.VMEM((lanes, both), F32),
-            pltpu.VMEM((2 * samples, channels, both), F32),
+            pltpu.VMEM((owned * lanes, both), F32),
+            pltpu.VMEM((owned * lanes, both), F32),
+            pltpu.VMEM((owned, 2 * samples, channels, both), F32),
         ],
         grid=(owned,),
         blocks={4: weight_block},
@@ -467,29 +474,25 @@
     arrived = exchange(send)
     steps = 4
     row_block = pl.BlockSpec((steps, lanes, width), lambda n: (n, 0, 0))
-    gate_rows, send = call(
+    gate_rows, send, local_sum = call(
         functools.partial(pixels_kernel, mode_scale, th),
         "pixels",
         (arrived, by_height, back_cols, forward_mix, field_rows, cot_rows, send_cols),
-        (field_shape, to_modes),
-        [pltpu.VMEM((inverse, owned * lanes), BF16)],
+        (field_shape, to_modes, shape((channels, channels), F32)),
+        [pltpu.VMEM((inverse, owned * lanes), BF16), pltpu.VMEM((lanes, lanes), F32)],
         grid=(th // steps,),
         blocks={4: row_block, 5: row_block},
         out_blocks={0: row_block, 1: pl.BlockSpec((halves, steps * lanes), lambda n: (0, n))},
+        limit=SMALL,
     )
     arrived = exchange(send)
-    (local_sum,) = call(
-        functools.partial(local_kernel, samples),
-        "local_grad",
-        (field_rows, gate_rows),
-        (shape((channels, channels), F32),),
-    )
     local_sum = sum_over(local_sum, "tile")
     (grad_spectra,) = call(
         functools.partial(grad_spectra_kernel, mode_scale, owned),
         "grad_spectra",
         (arrived, by_mode, rows, local_sum),
         (shape((owned * lanes + channels, both)),),
+        limit=SMALL,
     )
     all_grads = lax.all_gather(grad_spectra, "dp")
     (send,) = call(
@@ -497,7 +500,11 @@
         "mix_backward",
         (grad_spectra, back_rows, flat_weight),
         (to_pixels,),
-        [mixed, pltpu.VMEM((2 * samples, channels * ROWS, both), F32)],
+        [
+            pltpu.VMEM((owned * lanes, both), BF16),
+            pltpu.VMEM((owned * lanes, both), BF16),
+            pltpu.VMEM((owned, 2 * samples, channels * ROWS, both), F32),
+        ],
         grid=(owned,),
         blocks={2: weight_block},
     )
@@ -529,6 +536,7 @@
         (arrived, by_height, back_cols, backward_mix, gate_rows, by_channel),
         (shape((pixel_rows, width)),),
         [pltpu.VMEM((th, lanes, width), BF16)],
+        limit=SMALL,
     )
     return (input_grad.reshape(inputs.shape), mode_grad.reshape(mode_weight.shape), local_grad)
 

time: 144 us -> 138 us (0.958)
  Pallas kernels: 63.4 us -> 56.4 us
  waiting for transfers between devices: 19.1 us -> 23.8 us
  other arithmetic: 2.77 us -> 0.18 us
    pallas_call x9 -> x8, Pallas kernels: 63.4 us -> 56.4 us  [call(): pl.pallas_call(kernel, out_shape=tuple(outs), grid=grid, in_specs=in_spec...]
    ppermute x3, waiting for transfers between devices: 7.56 us -> 10.7 us  [sum_over(): lax.ppermute(values, axis, [(i, i ^ step) for i in range(size)])]
  transfers between devices with their start and end apart: 8 -> 8, of which waited for: 5 -> 5; matrix products, arithmetic and copies ran while one was open for 2% -> 0% of each run, Pallas kernels for 32% -> 29%
where the time goes in v1:
time: 138 us; the launch traced here: 137 us
  Pallas kernels  56.4 us (41%)
  waiting for transfers between devices  23.8 us (17%)
  blocking collectives  22 us (16%)
  starting transfers between devices  18.8 us (14%)
  between operations  14.1 us (10%)
    pallas_call x8, Pallas kernels, call(): pl.pallas_call(kernel, out_shape=tuple(outs), grid=grid, in_specs=in_spec...  56.4 us
    all_to_all x1, blocking collectives, exchange(): lax.all_to_all(split, 'tile', split_axis=0, concat_axis=0, tiled=False)  22 us
    all_to_all x3, starting transfers between devices, exchange(): lax.all_to_all(split, 'tile', split_axis=0, concat_axis=0, tiled=False)  13.7 us
    ppermute x3, waiting for transfers between devices, sum_over(): lax.ppermute(values, axis, [(i, i ^ step) for i in range(size)])  10.7 us
    all_to_all x3, waiting for transfers between devices, exchange(): lax.all_to_all(split, 'tile', split_axis=0, concat_axis=0, tiled=False)  10.6 us
    ppermute x3, starting transfers between devices, sum_over(): lax.ppermute(values, axis, [(i, i ^ step) for i in range(size)])  5.08 us
  transfers between devices with their start and end apart: 8, of which 5 were waited for; matrix products, arithmetic and copies ran while one was open for 0% of the time, Pallas kernels for 29%

profile of v1, /device:TPU:0, one launch (start us, length us, event | category | flops | bytes accessed | tf_op | source)
XLA Modules:
  0.0 136.8 jit_solution(15790047477464373256)
XLA Ops:
  7.2 2.9 %columns.1 = (bf16[16,128,256]{2,1,0:T(8,128)(2,1)}, bf16[128,2048]{1,0:T(8,128)(2,1)}) custom-call(bf16[256,256]{1,0:T(8,128)(2,1)} %constant.30.order_ref.restore_ref, bf16[128,256]{1,0:T(8,128)(2,1)} %constant.31.table_ref, bf16[2048,256]{1,0:T(8,128)(2,1)} %bitcast.21, bf16[2048,256]{1,0:T(8,128)(2,1)} %bitcast.22, bf16[2048,256]{1,0:T(8,128)(2,1)} %bitcast.23, ...), custom_call_target="tpu_custom_call" | custom-call | tf_op jit(solution)/shard_map/columns/pallas_call | solution.py:375
  10.1 0.0 copy-start.7
  10.1 0.0 copy-start.1
  10.1 0.0 copy-start.2
  10.1 0.0 copy-start.4
  10.1 0.0 copy-start.5
  10.1 22.0 %all_to_all.20 = bf16[8,16,2048]{2,1,0:T(8,128)(2,1)} all-to-all(bf16[8,16,2048]{2,1,0:T(8,128)(2,1)} %bitcast.36), channel_id=1, replica_groups=mesh['dp'=4,'tile'=8] {'tile'}, dimensions={0} | all-to-all | bytes 1048576 | tf_op jit(solution)/shard_map/all_to_all | solution.py:427
  32.1 0.0 copy-start.3
  32.1 0.0 copy-start.6
  32.1 11.0 %mix_forward.1 = (bf16[1024,128]{1,0:T(8,128)(2,1)}, bf16[256,1024]{1,0:T(8,128)(2,1)}) custom-call(bf16[128,2048]{1,0:T(8,128)(2,1)} %bitcast.32, bf16[128,128]{1,0:T(8,128)(2,1)} %constant.32.order_ref, bf16[256,128]{1,0:T(8,128)(2,1)} %constant.33.rows_ref, bf16[256,128]{1,0:T(8,128)(2,1)} %constant.34.back_ref, bf16[32768,128]{1,0:T(8,128)(2,1)} %bitcast.19), custom_call_target="tpu_custom_call" | custom-call | tf_op jit(solution)/shard_map/mix_forward/pallas_call | solution.py:375
  43.2 3.6 %all-to-all-start.1 = ((bf16[8,32,1024]{2,1,0:T(8,128)(2,1)}), bf16[8,32,1024]{2,1,0:T(8,128)(2,1)S(1)}, u32[]{:S(2)}, u32[]{:S(2)}) async-start(bf16[8,32,1024]{2,1,0:T(8,128)(2,1)} %bitcast.35), calls=%async_computation.1 | async-start | bytes 1048576 | tf_op jit(solution)/shard_map/all_to_all | solution.py:427
  46.7 0.0 all-gather.5.cloned.1.call-start
  46.8 0.7 all-gather.5.cloned.1.call-update
  47.5 2.6 %relayout.1.cot_ref = bf16[16,128,256]{2,1,0:T(8,128)(2,1)} custom-call(bf16[256,256]{1,0:T(8,128)(2,1)} %constant.30.order_ref.restore_ref, bf16[2048,256]{1,0:T(8,128)(2,1)} %bitcast.25, bf16[2048,256]{1,0:T(8,128)(2,1)} %bitcast.26, bf16[2048,256]{1,0:T(8,128)(2,1)} %bitcast.27, bf16[2048,256]{1,0:T(8,128)(2,1)} %bitcast.28), custom_call_target="tpu_custom_call" | custom-call | tf_op jit(solution)/shard_map/relayout/pallas_call | solution.py:375
  50.1 0.0 copy-done.7
  50.1 0.1 copy.15
  50.2 0.1 fusion.4.local_ref
  50.3 10.6 %all-to-all-done.1 = bf16[8,32,1024]{2,1,0:T(8,128)(2,1)S(1)} async-done(((bf16[8,32,1024]{2,1,0:T(8,128)(2,1)}), bf16[8,32,1024]{2,1,0:T(8,128)(2,1)S(1)}, u32[]{:S(2)}, u32[]{:S(2)}) %all-to-all-start.1) | async-done | bytes 524320 | tf_op jit(solution)/shard_map/all_to_all | solution.py:427
  60.9 0.0 copy-done.1
  60.9 0.0 copy-done.2
  60.9 0.0 copy-done.4
  60.9 0.0 copy-done.5
  60.9 0.0 copy-start
  61.0 1.2 copy-done
  62.2 6.6 %pixels.1 = (bf16[16,128,256]{2,1,0:T(8,128)(2,1)S(1)}, bf16[128,2048]{1,0:T(8,128)(2,1)}, f32[64,64]{1,0:T(8,128)S(1)}) custom-call(bf16[256,1024]{1,0:T(8,128)(2,1)S(1)} %bitcast.17, bf16[256,256]{1,0:T(8,128)(2,1)S(1)} %copy-done.1, bf16[128,256]{1,0:T(8,128)(2,1)S(1)} %copy-done.5, bf16[128,128]{1,0:T(8,128)(2,1)S(1)} %fusion.4.local_ref, ...), custom_call_target="tpu_custom_call" | custom-call | tf_op jit(solution)/shard_map/pixels/pallas_call | solution.py:375
  68.8 3.6 %all-to-all-start.2 = ((bf16[8,16,2048]{2,1,0:T(8,128)(2,1)}), bf16[8,16,2048]{2,1,0:T(8,128)(2,1)S(1)}, u32[]{:S(2)}, u32[]{:S(2)}) async-start(bf16[8,16,2048]{2,1,0:T(8,128)(2,1)} %bitcast.8), calls=%async_computation.2 | async-start | bytes 1048576 | tf_op jit(solution)/shard_map/all_to_all | solution.py:427
  72.5 0.0 all-gather.7.cloned.1.call-start
  72.5 2.0 %collective-permute-start = (f32[64,64]{1,0:T(8,128)S(1)}, f32[64,64]{1,0:T(8,128)S(1)}, u32[]{:S(2)}, u32[]{:S(2)}) collective-permute-start(f32[64,64]{1,0:T(8,128)S(1)} %get-tuple-element.18), channel_id=1, source_target_pairs={{0,1},{1,0},{2,3},{3,2},{4,5},{5,4},{6,7},{7,6},{8,9},{9,8},{10,11... | collective-permute-start | bytes 49160 | tf_op jit(solution)/shard_map/ppermute | solution.py:391
  74.5 4.7 %collective-permute-done = f32[64,64]{1,0:T(8,128)S(1)} collective-permute-done((f32[64,64]{1,0:T(8,128)S(1)}, f32[64,64]{1,0:T(8,128)S(1)}, u32[]{:S(2)}, u32[]{:S(2)}) %collective-permute-start) | collective-permute-done | bytes 16416 | tf_op jit(solution)/shard_map/ppermute | solution.py:391
  79.2 0.3 collective-permute-start.1
  79.5 4.0 %collective-permute-done.1 = f32[64,64]{1,0:T(8,128)S(1)} collective-permute-done((f32[64,64]{1,0:T(8,128)S(1)}, f32[64,64]{1,0:T(8,128)S(1)}, u32[]{:S(2)}, u32[]{:S(2)}) %collective-permute-start.1) | collective-permute-done | bytes 16416 | tf_op jit(solution)/shard_map/ppermute | solution.py:391
  83.5 2.8 %collective-permute-start.2 = (f32[64,64]{1,0:T(8,128)S(1)}, f32[64,64]{1,0:T(8,128)S(1)}, u32[]{:S(2)}, u32[]{:S(2)}) collective-permute-start(f32[64,64]{1,0:T(8,128)S(1)} %add.18), channel_id=1, source_target_pairs={{0,4},{1,5},{2,6},{3,7},{4,0},{5,1},{6,2},{7,3},{8,12},{9,13},{10,... | collective-permute-start | bytes 49160 | tf_op jit(solution)/shard_map/ppermute | solution.py:391
  86.3 2.0 %collective-permute-done.2 = f32[64,64]{1,0:T(8,128)S(1)} collective-permute-done((f32[64,64]{1,0:T(8,128)S(1)}, f32[64,64]{1,0:T(8,128)S(1)}, u32[]{:S(2)}, u32[]{:S(2)}) %collective-permute-start.2) | collective-permute-done | bytes 16416 | tf_op jit(solution)/shard_map/ppermute | solution.py:391
  88.3 0.0 all-to-all-done.2
  88.3 0.0 copy-done.3
  88.3 0.0 copy-done.6
  88.3 1.3 grad_spectra.1.spec_ref
  89.6 0.0 all-gather.7.cloned.1.call-update
  89.7 10.8 %mix_backward.1 = bf16[256,1024]{1,0:T(8,128)(2,1)} custom-call(bf16[1088,128]{1,0:T(8,128)(2,1)} %grad_spectra.1.spec_ref, bf16[256,128]{1,0:T(8,128)(2,1)} %constant.34.back_ref, bf16[32768,128]{1,0:T(8,128)(2,1)} %bitcast.20), custom_call_target="tpu_custom_call" | custom-call | tf_op jit(solution)/shard_map/mix_backward/pallas_call | solution.py:375
  100.4 6.5 %all-to-all-start.3 = ((bf16[8,32,1024]{2,1,0:T(8,128)(2,1)}), bf16[8,32,1024]{2,1,0:T(8,128)(2,1)S(1)}, u32[]{:S(2)}, u32[]{:S(2)}) async-start(bf16[8,32,1024]{2,1,0:T(8,128)(2,1)} %bitcast.31), calls=%async_computation.3 | async-start | bytes 1048576 | tf_op jit(solution)/shard_map/all_to_all | solution.py:427
  106.9 0.1 fusion.5.local_ref
  107.0 0.0 all-gather.5.cloned.1.call-done
  107.0 1.8 %all-gather.7.cloned.1.call-done = bf16[4352,128]{1,0:T(8,128)(2,1)} async-done(((bf16[1088,128]{1,0:T(8,128)(2,1)}), bf16[4352,128]{1,0:T(8,128)(2,1)}) %all-gather.7.cloned.1.call-update) | async-done | bytes 1114128 | tf_op jit(solution)/shard_map/all_gather | solution.py:497
  108.8 18.8 %mode_grad.1 = (f32[32768,128]{1,0:T(8,128)}, f32[64,64]{1,0:T(8,128)}) custom-call(bf16[4,1024,128]{2,1,0:T(8,128)(2,1)} %bitcast.33, bf16[4,1088,128]{2,1,0:T(8,128)(2,1)} %bitcast.29, bf16[4,1088,128]{2,1,0:T(8,128)(2,1)} %bitcast.30), custom_call_target="tpu_custom_call" | custom-call | tf_op jit(solution)/shard_map/mode_grad/pallas_call | solution.py:375
  127.6 0.0 all-to-all-done.3
  127.6 2.3 %final.1 = bf16[2048,256]{1,0:T(8,128)(2,1)} custom-call(bf16[256,1024]{1,0:T(8,128)(2,1)S(1)} %bitcast.18, bf16[256,256]{1,0:T(8,128)(2,1)S(1)} %copy-done.1, bf16[128,256]{1,0:T(8,128)(2,1)S(1)} %copy-done.5, bf16[128,128]{1,0:T(8,128)(2,1)S(1)} %fusion.5.local_ref, bf16[16,128,256]{2,1,0:T(8,128)(2,1)S(1)} %get-tuple-element.22.grad_ref, ...), custom_call_target="tpu_custom_call" | custom-call | tf_op jit(solution)/shard_map/final/pallas_call | solution.py:375
  (3 shorter events, 0.0 us)
Async XLA Ops:
  10.1 40.1 %copy-start.7 = (bf16[64,64]{1,0:T(8,128)(2,1)S(1)}, bf16[64,64]{1,0:T(8,128)(2,1)}, u32[]{:S(2)}) copy-start(bf16[64,64]{1,0:T(8,128)(2,1)} %param.15) | copy-start | bytes 24580
  10.1 50.9 %copy-start.1 = (bf16[256,256]{1,0:T(8,128)(2,1)S(1)}, bf16[256,256]{1,0:T(8,128)(2,1)}, u32[]{:S(2)}) copy-start(bf16[256,256]{1,0:T(8,128)(2,1)} %constant.30.order_ref.restore_ref) | copy-start | bytes 393220
  10.1 50.9 %copy-start.2 = (bf16[16,128,256]{2,1,0:T(8,128)(2,1)S(1)}, bf16[16,128,256]{2,1,0:T(8,128)(2,1)}, u32[]{:S(2)}) copy-start(bf16[16,128,256]{2,1,0:T(8,128)(2,1)} %get-tuple-element.16.field_ref) | copy-start | bytes 3145732
  10.1 50.9 %copy-start.4 = (bf16[128,256]{1,0:T(8,128)(2,1)S(1)}, bf16[128,256]{1,0:T(8,128)(2,1)}, u32[]{:S(2)}) copy-start(bf16[128,256]{1,0:T(8,128)(2,1)} %constant.31.table_ref) | copy-start | bytes 196612
  10.1 50.9 %copy-start.5 = (bf16[128,256]{1,0:T(8,128)(2,1)S(1)}, bf16[128,256]{1,0:T(8,128)(2,1)}, u32[]{:S(2)}) copy-start(bf16[128,256]{1,0:T(8,128)(2,1)} %constant.35.back_ref) | copy-start | bytes 196612
  32.1 56.2 %copy-start.3 = (bf16[256,128]{1,0:T(8,128)(2,1)S(1)}, bf16[256,128]{1,0:T(8,128)(2,1)}, u32[]{:S(2)}) copy-start(bf16[256,128]{1,0:T(8,128)(2,1)} %constant.33.rows_ref) | copy-start | bytes 196612
  32.1 56.2 %copy-start.6 = (bf16[128,128]{1,0:T(8,128)(2,1)S(1)}, bf16[128,128]{1,0:T(8,128)(2,1)}, u32[]{:S(2)}) copy-start(bf16[128,128]{1,0:T(8,128)(2,1)} %constant.32.order_ref) | copy-start | bytes 98308
  43.2 17.8 %all-to-all-start.1 = ((bf16[8,32,1024]{2,1,0:T(8,128)(2,1)}), bf16[8,32,1024]{2,1,0:T(8,128)(2,1)S(1)}, u32[]{:S(2)}, u32[]{:S(2)}) async-start(bf16[8,32,1024]{2,1,0:T(8,128)(2,1)} %bitcast.35), calls=%async_computation.1 | async-start | bytes 1048576 | tf_op jit(solution)/shard_map/all_to_all | solution.py:427
  46.7 60.2 %all-gather.5.cloned.1.call-start = ((), (), s32[]{:S(2)}) async-start(), calls=%async_computation.4 | async-start | bytes 1310720 | tf_op jit(solution)/shard_map/all_gather | solution.py:473
  60.9 1.2 copy-start
  68.8 19.5 %all-to-all-start.2 = ((bf16[8,16,2048]{2,1,0:T(8,128)(2,1)}), bf16[8,16,2048]{2,1,0:T(8,128)(2,1)S(1)}, u32[]{:S(2)}, u32[]{:S(2)}) async-start(bf16[8,16,2048]{2,1,0:T(8,128)(2,1)} %bitcast.8), calls=%async_computation.2 | async-start | bytes 1048576 | tf_op jit(solution)/shard_map/all_to_all | solution.py:427
  72.5 36.3 %all-gather.7.cloned.1.call-start = ((), (), s32[]{:S(2)}) async-start(), calls=%async_computation.5 | async-start | bytes 1392640 | tf_op jit(solution)/shard_map/all_gather | solution.py:497
  72.5 6.7 %collective-permute-start = (f32[64,64]{1,0:T(8,128)S(1)}, f32[64,64]{1,0:T(8,128)S(1)}, u32[]{:S(2)}, u32[]{:S(2)}) collective-permute-start(f32[64,64]{1,0:T(8,128)S(1)} %get-tuple-element.18), channel_id=1, source_target_pairs={{0,1},{1,0},{2,3},{3,2},{4,5},{5,4},{6,7},{7,6},{8,9},{9,8},{10,11... | collective-permute-start | bytes 49160 | tf_op jit(solution)/shard_map/ppermute | solution.py:391
  79.2 4.3 %collective-permute-start.1 = (f32[64,64]{1,0:T(8,128)S(1)}, f32[64,64]{1,0:T(8,128)S(1)}, u32[]{:S(2)}, u32[]{:S(2)}) collective-permute-start(f32[64,64]{1,0:T(8,128)S(1)} %add.17), channel_id=1, source_target_pairs={{0,2},{1,3},{2,0},{3,1},{4,6},{5,7},{6,4},{7,5},{8,10},{9,11},{10,... | collective-permute-start | bytes 49160 | tf_op jit(solution)/shard_map/ppermute | solution.py:391
  83.5 4.8 %collective-permute-start.2 = (f32[64,64]{1,0:T(8,128)S(1)}, f32[64,64]{1,0:T(8,128)S(1)}, u32[]{:S(2)}, u32[]{:S(2)}) collective-permute-start(f32[64,64]{1,0:T(8,128)S(1)} %add.18), channel_id=1, source_target_pairs={{0,4},{1,5},{2,6},{3,7},{4,0},{5,1},{6,2},{7,3},{8,12},{9,13},{10,... | collective-permute-start | bytes 49160 | tf_op jit(solution)/shard_map/ppermute | solution.py:391
  100.4 27.2 %all-to-all-start.3 = ((bf16[8,32,1024]{2,1,0:T(8,128)(2,1)}), bf16[8,32,1024]{2,1,0:T(8,128)(2,1)S(1)}, u32[]{:S(2)}, u32[]{:S(2)}) async-start(bf16[8,32,1024]{2,1,0:T(8,128)(2,1)} %bitcast.31), calls=%async_computation.3 | async-start | bytes 1048576 | tf_op jit(solution)/shard_map/all_to_all | solution.py:427
Sparse Core Ops, SparseCore 0:
  49.1 18.1 all-gather.4
  89.8 18.9 all-gather.6
